TPU v7x, 32 devices: a whole 2x2x4 slice. The times are simulated.
32 devices in a mesh: ga: 2 (over y), aa: 4 (over x, core), ba: 4 (over z).
Axes of the slice: x: 2, y: 2, z: 4, core: 2. Of those that a mesh axis runs over, the one named last changes fastest.
Arguments:
- query: bfloat16 [2048, 5120], P(('ga', 'aa'), 'ba'), parts along dimension 0, may hold values from -64 to 64
- keys: bfloat16 [16384, 1024], P(('ga', 'aa'), 'ba'), parts along dimension 0, may hold values from -16 to 16
- values: bfloat16 [16384, 1024], P(('ga', 'aa'), 'ba'), parts along dimension 0, may hold values from -6 to 6
- cache_lengths: int32 [8], P(('ga', 'aa')), parts along dimension 0, may hold values from 256 to 2048, as said below
- residual: bfloat16 [2048, 5120], P(('ga', 'ba'), 'aa'), parts along dimension 0, may hold values from -16 to 16
- out_weight: bfloat16 [5120, 5120], P('ba', 'aa'), may hold values from -0.078125 to 0.078125
- norm_gain: float32 [5120], P('aa'), may hold values from 0.1 to 1.9
- router_weight: float32 [5120, 4], P('aa'), may hold values from -0.078125 to 0.078125
- expert_ids: int32 [2048], P(('ga', 'ba')), parts along dimension 0, may hold values from 0 to 3
- expert_slots: int32 [2048], P(('ga', 'ba')), parts along dimension 0, may hold values from -1 to 127, as said below
- expert_gate: bfloat16 [4, 5120, 4096], P('ba', None, 'aa'), may hold values from -0.078125 to 0.078125
- expert_up: bfloat16 [4, 5120, 4096], P('ba', None, 'aa'), may hold values from -0.078125 to 0.078125
- expert_down: bfloat16 [4, 4096, 5120], P('ba', 'aa'), may hold values from -0.25 to 0.25
Outputs:
- layer_out: bfloat16 [2048, 5120], P(('ga', 'ba'), 'aa'), parts along dimension 0
There are 2 independent parts, one for each index of `ga`. A program takes and returns all parts, laid end to end along the dimension named above; an argument that names none is the same for every part. Nothing has to cross between parts.
Inputs may be any that keep to these rules, and one draw needn't show every extreme that they name: `cache_lengths`: some shard has 2048 valid positions in every draw. `expert_slots`: rows form aligned blocks of 256 rows (the rows of one index of ba). A row's slot is the number of earlier rows of its block with the same expert id, or -1 where that number is 128 or more. In every draw some expert has all 128 slots filled in every block.
All inputs are finite; a program needn't handle non-finite values.
Results may differ from a plain program's by a relative error of at most 0.019.
Values may be sent and summed in bfloat16 or wider, within the bound.
No kernel may reach another device: no remote copies, remote signals or barrier semaphores. Data moves between devices by JAX's collectives and lax.ppermute only.
A program may use at most 128 MiB of HBM per device.

v0:
```python
import jax
import jax.numpy as jnp
from jax import lax
from jax.sharding import PartitionSpec as P

D = 5120
HD = 128
Q = 1024
CTX_DEV = 2048


NEGATIVE = -1e30
EPSILON = 1e-05


def head_partials(rows, key_block, value_block, length):
    heads = rows.shape[1] // HD
    kv_heads = key_block.shape[1] // HD
    group = heads // kv_heads
    valid = lax.broadcasted_iota(jnp.int32, (1, key_block.shape[0]), 1) < length
    maxima = []
    totals = []
    outputs = []
    for head in range(heads):
        source = head // group
        q_head = rows[:, head * HD : (head + 1) * HD]
        k_head = key_block[:, source * HD : (source + 1) * HD]
        v_head = value_block[:, source * HD : (source + 1) * HD]
        scores = lax.dot_general(
            q_head, k_head, (((1,), (1,)), ((), ())), preferred_element_type=jnp.float32
        ) * HD ** (-0.5)
        scores = jnp.where(valid, scores, NEGATIVE)
        peak = jnp.max(scores, axis=1)
        probs = jnp.exp(scores - peak[:, None])
        maxima.append(peak)
        totals.append(jnp.sum(probs, axis=1))
        outputs.append(
            jnp.dot(probs.astype(jnp.bfloat16), v_head, preferred_element_type=jnp.float32)
        )
    return (jnp.stack(maxima, axis=1), jnp.stack(totals, axis=1), jnp.concatenate(outputs, axis=1))


def combine_partials(first, second):
    peak_one, total_one, out_one = first
    peak_two, total_two, out_two = second
    peak = jnp.maximum(peak_one, peak_two)
    scale_one = jnp.exp(peak_one - peak)
    scale_two = jnp.exp(peak_two - peak)
    outputs = out_one * jnp.repeat(scale_one, HD, axis=1) + out_two * jnp.repeat(
        scale_two, HD, axis=1
    )
    return (peak, total_one * scale_one + total_two * scale_two, outputs)


def on_device(
    query,
    keys,
    values,
    cache_lengths,
    residual,
    out_weight,
    norm_gain,
    router_weight,
    expert_ids,
    expert_slots,
    expert_gate,
    expert_up,
    expert_down,
):
    heads = query.shape[1] // HD
    own_rows = query.shape[0]
    start_state = (
        jnp.full((own_rows, heads), NEGATIVE, jnp.float32),
        jnp.zeros((own_rows, heads), jnp.float32),
        jnp.zeros((own_rows, heads * HD), jnp.float32),
    )
    key_piece = lax.all_gather(keys, "aa", axis=0, tiled=True)
    value_piece = lax.all_gather(values, "aa", axis=0, tiled=True)
    length_piece = lax.all_gather(cache_lengths, "aa", axis=0, tiled=True)

    def one_shard(index, carry):
        key_block = lax.dynamic_slice_in_dim(key_piece, index * CTX_DEV, CTX_DEV, 0)
        value_block = lax.dynamic_slice_in_dim(value_piece, index * CTX_DEV, CTX_DEV, 0)
        return combine_partials(
            carry, head_partials(query, key_block, value_block, length_piece[index])
        )

    peak, total, weighted = lax.fori_loop(0, length_piece.shape[0], one_shard, start_state)
    own = (weighted / jnp.repeat(total, HD, axis=1)).astype(jnp.bfloat16)
    attended = lax.all_gather(own, "aa", axis=0, tiled=True)
    hidden = residual.astype(jnp.float32) + lax.psum_scatter(
        jnp.dot(attended, out_weight, preferred_element_type=jnp.float32).astype(jnp.bfloat16),
        "ba",
        scatter_dimension=0,
        tiled=True,
    ).astype(jnp.float32)
    squares = lax.psum(jnp.sum(hidden * hidden, axis=1), "aa")
    inverse = 1.0 / jnp.sqrt(squares / D + EPSILON)
    normed = hidden * inverse[:, None] * norm_gain
    logits = lax.psum(jnp.dot(normed, router_weight, precision=lax.Precision.HIGHEST), "aa")
    experts = router_weight.shape[1]
    chosen = expert_ids[:, None] == lax.broadcasted_iota(jnp.int32, (1, experts), 1)
    gate = jnp.sum(jnp.where(chosen, jax.nn.sigmoid(logits), 0.0), axis=1)
    expert_in = normed.astype(jnp.bfloat16)
    slot_count = 2 * Q // (lax.axis_size("ba") * experts)
    combined = expert_ids * slot_count + expert_slots
    placing = (
        combined[:, None] == lax.broadcasted_iota(jnp.int32, (1, experts * slot_count), 1)
    ) & (expert_slots[:, None] >= 0)
    placing = placing.astype(jnp.bfloat16)
    packed = lax.dot_general(
        placing, expert_in, (((0,), (0,)), ((), ())), preferred_element_type=jnp.float32
    ).astype(jnp.bfloat16)
    arrived = lax.all_to_all(packed, "ba", split_axis=0, concat_axis=0, tiled=True)
    gate_w = expert_gate[0]
    up_w = expert_up[0]
    down_w = expert_down[0]
    piece = lax.all_gather(arrived, "aa", axis=1, tiled=True)
    gate_part = jnp.dot(piece, gate_w, preferred_element_type=jnp.float32)
    up_part = jnp.dot(piece, up_w, preferred_element_type=jnp.float32)
    act = (jax.nn.silu(gate_part) * up_part).astype(jnp.bfloat16)
    expert_out = lax.psum_scatter(
        lax.dot_general(
            down_w, act, (((0,), (1,)), ((), ())), preferred_element_type=jnp.float32
        ).astype(jnp.bfloat16),
        "aa",
        scatter_dimension=0,
        tiled=True,
    )
    returned = lax.all_to_all(expert_out, "ba", split_axis=1, concat_axis=1, tiled=True)
    from_experts = lax.dot_general(
        placing, returned, (((1,), (1,)), ((), ())), preferred_element_type=jnp.float32
    )
    return (hidden + gate[:, None] * from_experts).astype(jnp.bfloat16)


def solution(mesh):
    return jax.shard_map(
        on_device,
        mesh=mesh,
        in_specs=(
            P(("ga", "aa"), "ba"),
            P(("ga", "aa"), "ba"),
            P(("ga", "aa"), "ba"),
            P(("ga", "aa")),
            P(("ga", "ba"), "aa"),
            P("ba", "aa"),
            P("aa"),
            P("aa", None),
            P(("ga", "ba")),
            P(("ga", "ba")),
            P("ba", None, "aa"),
            P("ba", None, "aa"),
            P("ba", "aa", None),
        ),
        out_specs=P(("ga", "ba"), "aa"),
        check_vma=False,
    )
```

profile of v0, /device:TPU:26, one launch (start us, length us, event | category | flops | bytes accessed | tf_op | source)
XLA Modules:
  0.0 469.4 jit_solution(9405329389665705424)
XLA Ops:
  10.1 4.3 all-reduce
  14.3 29.1 %all-gather.5.cloned.1.call-done = bf16[8192,256]{1,0:T(8,128)(2,1)} async-done(((bf16[2048,256]{1,0:T(8,128)(2,1)}), bf16[8192,256]{1,0:T(8,128)(2,1)}) %all-gather.5.cloned.1.call-update) | async-done | bytes 4194320 | tf_op jit(solution)/shard_map/all_gather | solution.py:77
  43.5 36.1 %all-gather.7.cloned.1.call-done = bf16[8192,256]{1,0:T(8,128)(2,1)} async-done(((bf16[2048,256]{1,0:T(8,128)(2,1)}), bf16[8192,256]{1,0:T(8,128)(2,1)}) %all-gather.7.cloned.1.call-update) | async-done | bytes 4194320 | tf_op jit(solution)/shard_map/all_gather | solution.py:78
  79.6 92.8 %while.18 = (s32[]{:T(128)}, f32[256,10]{0,1:T(8,128)S(1)}, f32[256,10]{0,1:T(8,128)S(1)}, f32[256,1280]{0,1:T(8,128)}, s32[4]{0:T(128)S(1)}, /*index=5*/bf16[81...) while((s32[]{:T(128)}, f32[256,10]{0,1:T(8,128)S(1)}, ...), condition=%wide.region_21.22_spmd.clone, body=%wide.region_0.21_spmd.clone.sunk | while | flops 2722382848 | bytes 120924600 | solution.py:88
  99.9 2.6 fusion.227
  122.8 3.0 fusion.227
  146.1 3.0 fusion.227
  169.4 3.0 fusion.227
  172.4 2.3 fusion.110
  174.7 26.0 %all-gather.9.cloned.1.call-done = bf16[1024,1280]{0,1:T(8,128)(2,1)} async-done(((bf16[256,1280]{0,1:T(8,128)(2,1)}), bf16[1024,1280]{0,1:T(8,128)(2,1)}) %all-gather.9.cloned.1.call-update) | async-done | bytes 2621456 | tf_op jit(solution)/shard_map/all_gather | solution.py:90
  200.7 6.9 %convolution_convert_fusion = bf16[1024,1280]{1,0:T(8,128)(2,1)} fusion(bf16[1024,1280]{0,1:T(8,128)(2,1)} %all-gather.9.cloned.1.call-done, bf16[1280,1280]{1,0:T(8,128)(2,1)S(1)} %copy-done), kind=kOutput, calls=%fused_computation.127 | convolution fusion | flops 3356753920 | bytes 8519680 | tf_op jit(solution)/shard_map/dot_general | solution.py:92
  208.3 51.2 %reduce-scatter.3.cloned.1.call-done = bf16[256,1280]{1,0:T(8,128)(2,1)} async-done(((bf16[1024,1280]{1,0:T(8,128)(2,1)}), bf16[256,1280]{1,0:T(8,128)(2,1)}) %reduce-scatter.3.cloned.1.call-update) | async-done | bytes 655376 | tf_op jit(solution)/shard_map/reduce_scatter | solution.py:91
  260.8 5.8 %psum.14 = f32[256]{0:T(256)S(1)} all-reduce(f32[256]{0:T(256)S(1)} %multiply_reduce_fusion), channel_id=1, replica_groups=mesh['ga'=2,'aa'=4,'ba'=4] {'aa'}, use_global_device_ids=true, to_apply=%region_24.25 | all-reduce | flops 256 | bytes 2048 | tf_op jit(solution)/shard_map/psum | solution.py:97
  266.6 1.9 convolution_convert_fusion.1
  268.5 34.2 %all_to_all.24 = bf16[4,128,1280]{2,1,0:T(8,128)(2,1)} all-to-all(bf16[4,128,1280]{2,1,0:T(8,128)(2,1)S(1)} %bitcast.111), channel_id=1, replica_groups=mesh['ga'=2,'aa'=4,'ba'=4] {'ba'}, dimensions={0} | all-to-all | bytes 2621440 | tf_op jit(solution)/shard_map/all_to_all | solution.py:114
  302.7 40.5 %all-gather.11.cloned.1.call-done = bf16[512,5120]{1,0:T(8,128)(2,1)} async-done(((bf16[512,1280]{1,0:T(8,128)(2,1)}), bf16[512,5120]{1,0:T(8,128)(2,1)}) %all-gather.11.cloned.1.call-update) | async-done | bytes 5242896 | tf_op jit(solution)/shard_map/all_gather | solution.py:118
  343.3 9.9 %fusion.94 = f32[512,1024]{1,0:T(8,128)S(1)} fusion(bf16[512,5120]{1,0:T(8,128)(2,1)} %all-gather.11.cloned.1.call-done, bf16[1,5120,1024]{2,1,0:T(8,128)(2,1)} %param.26), kind=kOutput, calls=%fused_computation.121 | convolution fusion | flops 5368709120 | bytes 17825792 | tf_op jit(solution)/shard_map/dot_general | solution.py:120
  353.2 20.6 %fusion.101 = bf16[5120,512]{0,1:T(8,128)(2,1)} fusion(bf16[1,1024,5120]{2,1,0:T(8,128)(2,1)} %param.27, f32[512,1024]{1,0:T(8,128)S(1)} %fusion.94, bf16[512,5120]{1,0:T(8,128)(2,1)} %all-gather.11.cloned.1.call-done, bf16[1,5120,1024]{2,1,0:T(8,128)(2,1)} %param.25), kind=kOutput, calls=%fused_computation.126 | convolution fusion | flops 10743185408 | bytes 33554432 | tf_op jit(solution)/shard_map/dot_general | solution.py:123
  373.8 51.5 %reduce-scatter.5.cloned.1.call-done = bf16[1280,512]{0,1:T(8,128)(2,1)} async-done(((bf16[5120,512]{0,1:T(8,128)(2,1)}), bf16[1280,512]{0,1:T(8,128)(2,1)}) %reduce-scatter.5.cloned.1.call-update) | async-done | bytes 1310736 | tf_op jit(solution)/shard_map/reduce_scatter | solution.py:122
  425.3 5.1 %all-to-all-start.1 = ((bf16[1280,4,128]{0,2,1:T(8,128)(2,1)}), bf16[1280,4,128]{0,2,1:T(8,128)(2,1)}, u32[]{:S(2)}, u32[]{:S(2)}) async-start(bf16[1280,4,128]{0,2,1:T(8,128)(2,1)} %bitcast.110), calls=%async_computation.3 | async-start | bytes 2621440 | tf_op jit(solution)/shard_map/all_to_all | solution.py:130
  430.4 2.7 fusion.112
  433.1 6.4 %psum.15 = f32[256,4]{0,1:T(4,128)S(1)} all-reduce(f32[256,4]{0,1:T(4,128)S(1)} %fusion.112), channel_id=1, replica_groups=mesh['ga'=2,'aa'=4,'ba'=4] {'aa'}, use_global_device_ids=true, to_apply=%region_25.26 | all-reduce | flops 1024 | bytes 8192 | tf_op jit(solution)/shard_map/psum | solution.py:100
  439.6 19.9 %all-to-all-done.1 = bf16[1280,4,128]{0,2,1:T(8,128)(2,1)} async-done(((bf16[1280,4,128]{0,2,1:T(8,128)(2,1)}), bf16[1280,4,128]{0,2,1:T(8,128)(2,1)}, u32[]{:S(2)}, u32[]{:S(2)}) %all-to-all-start.1) | async-done | bytes 1310752 | tf_op jit(solution)/shard_map/all_to_all | solution.py:130
  459.5 3.1 fusion.105
  (211 shorter events, 85.7 us)
Async XLA Ops:
  6.5 194.2 %copy-start = (bf16[1280,1280]{1,0:T(8,128)(2,1)S(1)}, bf16[1280,1280]{1,0:T(8,128)(2,1)}, u32[]{:S(2)}) copy-start(bf16[1280,1280]{1,0:T(8,128)(2,1)} %param.20) | copy-start | bytes 9830404
  6.5 2.2 copy-start.11
  6.5 36.9 %all-gather.5.cloned.1.call-start = ((), (), s32[]{:S(2)}) async-start(), calls=%async_computation.4 | async-start | bytes 5242880 | tf_op jit(solution)/shard_map/all_gather | solution.py:77
  7.3 72.3 %all-gather.7.cloned.1.call-start = ((), (), s32[]{:S(2)}) async-start(), calls=%async_computation.5 | async-start | bytes 5242880 | tf_op jit(solution)/shard_map/all_gather | solution.py:78
  8.0 192.7 %all-gather.9.cloned.1.call-start = ((), (), s32[]{:S(2)}) async-start(), calls=%async_computation.6 | async-start | bytes 3276800 | tf_op jit(solution)/shard_map/all_gather | solution.py:90
  80.7 2.4 copy-start.2
  83.1 1.8 copy-start.5
  91.4 2.2 copy-start.3
  103.6 2.4 copy-start.2
  106.0 1.8 copy-start.5
  114.4 2.2 copy-start.3
  126.9 2.4 copy-start.2
  137.7 2.2 copy-start.3
  150.2 2.4 copy-start.2
  152.6 1.8 copy-start.5
  161.0 2.2 copy-start.3
  174.6 84.8 %reduce-scatter.3.cloned.1.call-start = ((), (), s32[]{:S(2)}) async-start(), calls=%async_computation.7 | async-start | bytes 3276800 | tf_op jit(solution)/shard_map/reduce_scatter | solution.py:91
  207.6 51.9 %copy-start.6 = (bf16[256,1280]{1,0:T(8,128)(2,1)S(1)}, bf16[256,1280]{1,0:T(8,128)(2,1)}, u32[]{:S(2)}) copy-start(bf16[256,1280]{1,0:T(8,128)(2,1)} %param.19) | copy-start | bytes 1966084
  207.6 59.0 %copy-start.10 = (f32[1280]{0:T(1024)S(1)}, f32[1280]{0:T(1024)}, u32[]{:S(2)}) copy-start(f32[1280]{0:T(1024)} %param.21) | copy-start | bytes 15364
  207.6 135.7 %all-gather.11.cloned.1.call-start = ((), (), s32[]{:S(2)}) async-start(), calls=%async_computation.8 | async-start | bytes 6553600 | tf_op jit(solution)/shard_map/all_gather | solution.py:118
  302.7 122.6 %reduce-scatter.5.cloned.1.call-start = ((), (), s32[]{:S(2)}) async-start(), calls=%async_computation.9 | async-start | bytes 6553600 | tf_op jit(solution)/shard_map/reduce_scatter | solution.py:122
  373.8 56.6 %copy-start.9 = (f32[1280,4]{0,1:T(4,128)S(1)}, f32[1280,4]{0,1:T(4,128)}, u32[]{:S(2)}) copy-start(f32[1280,4]{0,1:T(4,128)} %param.22) | copy-start | bytes 61444
  425.3 34.2 %all-to-all-start.1 = ((bf16[1280,4,128]{0,2,1:T(8,128)(2,1)}), bf16[1280,4,128]{0,2,1:T(8,128)(2,1)}, u32[]{:S(2)}, u32[]{:S(2)}) async-start(bf16[1280,4,128]{0,2,1:T(8,128)(2,1)} %bitcast.110), calls=%async_computation.3 | async-start | bytes 2621440 | tf_op jit(solution)/shard_map/all_to_all | solution.py:130
  430.4 32.2 %copy-start.1 = (bf16[1280,1280]{1,0:T(8,128)(2,1)S(1)}, bf16[1280,1280]{1,0:T(8,128)(2,1)}, u32[]{:S(2)}) copy-start(bf16[1280,1280]{1,0:T(8,128)(2,1)} %param.20) | copy-start | bytes 9830404
  (7 other events, 7.9 us)
Sparse Core Ops, SparseCore 0:
  8.9 34.5 all-gather.4
  45.0 34.4 all-gather.6
  174.8 25.8 all-gather.8
  207.7 51.6 reduce-scatter.2
  302.8 40.4 all-gather.10
  373.9 51.3 reduce-scatter.4
where the time goes:
time: 475 us; the launch traced here: 469 us
  waiting for transfers between devices  256 us (54%)
  matrix products  96 us (20%)
  blocking collectives  50.6 us (11%)
  other arithmetic  32.1 us (7%)
  local copies, waits for them, and re-layouts  14.9 us (3%)
  between operations  14.2 us (3%)
  starting transfers between devices  5.3 us (1%)
    reduce_scatter x1, waiting for transfers between devices, on_device(): lax.psum_scatter(lax.dot_general(down_w, act, (((0,), (1,)), ((), ())), p...  51.5 us
    reduce_scatter x1, waiting for transfers between devices, on_device(): lax.psum_scatter(jnp.dot(attended, out_weight, preferred_element_type=jnp...  51.2 us
    all_gather x1, waiting for transfers between devices, on_device(): piece = lax.all_gather(arrived, 'aa', axis=1, tiled=True)  40.5 us
    all_gather x1, waiting for transfers between devices, on_device(): value_piece = lax.all_gather(values, 'aa', axis=0, tiled=True)  36.1 us
    all_to_all x1, blocking collectives, on_device(): lax.all_to_all(packed, 'ba', split_axis=0, concat_axis=0, tiled=True)  34.2 us
    dot_general x40, matrix products, head_partials(): lax.dot_general(q_head, k_head, (((1,), (1,)), ((), ())), preferred_eleme...  31.5 us
    all_gather x1, waiting for transfers between devices, on_device(): key_piece = lax.all_gather(keys, 'aa', axis=0, tiled=True)  29.1 us
    all_gather x1, waiting for transfers between devices, on_device(): attended = lax.all_gather(own, 'aa', axis=0, tiled=True)  26 us
  transfers between devices with their start and end apart: 7, of which 7 were waited for; matrix products, arithmetic and copies ran while one was open for 1% of the time, Pallas kernels for 0%

commit v1 on v0

--- a/solution.py
+++ b/solution.py
@@ -1,16 +1,19 @@
+import functools
+import math
+
 import jax
 import jax.numpy as jnp
 from jax import lax
+from jax.experimental import pallas as pl
+from jax.experimental.pallas import tpu as pltpu
 from jax.sharding import PartitionSpec as P
 
-D = 5120
 HD = 128
-Q = 1024
-CTX_DEV = 2048
-
-
+KEY_BLOCK = 512
 NEGATIVE = -1e30
 EPSILON = 1e-05
+SCALE = HD ** (-0.5)
+SCALE_LOG2 = SCALE * math.log2(math.e)
 
 
 def head_partials(rows, key_block, value_block, length):
@@ -28,7 +31,7 @@
         v_head = value_block[:, source * HD : (source + 1) * HD]
         scores = lax.dot_general(
             q_head, k_head, (((1,), (1,)), ((), ())), preferred_element_type=jnp.float32
-        ) * HD ** (-0.5)
+        ) * SCALE
         scores = jnp.where(valid, scores, NEGATIVE)
         peak = jnp.max(scores, axis=1)
         probs = jnp.exp(scores - peak[:, None])
@@ -50,6 +53,223 @@
         scale_two, HD, axis=1
     )
     return (peak, total_one * scale_one + total_two * scale_two, outputs)
+
+
+def plain_projection(query, keys, values, cache_lengths, out_weight):
+    heads = query.shape[1] // HD
+    own_rows = query.shape[0]
+    context = keys.shape[0]
+    start_state = (
+        jnp.full((own_rows, heads), NEGATIVE, jnp.float32),
+        jnp.zeros((own_rows, heads), jnp.float32),
+        jnp.zeros((own_rows, heads * HD), jnp.float32),
+    )
+    key_piece = lax.all_gather(keys, "aa", axis=0, tiled=True)
+    value_piece = lax.all_gather(values, "aa", axis=0, tiled=True)
+    length_piece = lax.all_gather(cache_lengths, "aa", axis=0, tiled=True)
+
+    def one_shard(index, carry):
+        key_block = lax.dynamic_slice_in_dim(key_piece, index * context, context, 0)
+        value_block = lax.dynamic_slice_in_dim(value_piece, index * context, context, 0)
+        return combine_partials(
+            carry, head_partials(query, key_block, value_block, length_piece[index])
+        )
+
+    peak, total, weighted = lax.fori_loop(0, length_piece.shape[0], one_shard, start_state)
+    own = (weighted / jnp.repeat(total, HD, axis=1)).astype(jnp.bfloat16)
+    attended = lax.all_gather(own, "aa", axis=0, tiled=True)
+    return lax.psum_scatter(
+        jnp.dot(attended, out_weight, preferred_element_type=jnp.float32).astype(jnp.bfloat16),
+        "ba",
+        scatter_dimension=0,
+        tiled=True,
+    ).astype(jnp.float32)
+
+
+def attend_body(*refs, shards, units, resume, finish, block):
+    lengths, q_ref = refs[0], refs[1]
+    kv_refs = refs[2 : 2 + shards]
+    at = 2 + shards
+    if resume:
+        peak_in, sums_in = refs[at : at + 2]
+        at += 2
+    if finish:
+        out_ref, peak, sums = refs[at : at + 3]
+    else:
+        peak, sums = refs[at : at + 2]
+    if resume:
+        peak[...] = peak_in[...]
+        sums[...] = sums_in[...]
+    else:
+        peak[...] = jnp.full(peak.shape, NEGATIVE, jnp.float32)
+        sums[...] = jnp.zeros(sums.shape, jnp.float32)
+
+    def one_block(kv_ref, base, length, tail):
+        key = kv_ref[pl.ds(base, block), :HD]
+        value = kv_ref[pl.ds(base, block), HD:]
+        ones = jnp.ones((block, HD), jnp.bfloat16)
+        if tail:
+            valid = base + lax.broadcasted_iota(jnp.int32, (block, HD), 0) < length
+            first = kv_ref[0:1, :HD].astype(jnp.float32)
+            key = jnp.where(valid, key.astype(jnp.float32), first).astype(jnp.bfloat16)
+            value = jnp.where(valid, value.astype(jnp.float32), 0.0).astype(jnp.bfloat16)
+            ones = jnp.where(valid, 1.0, 0.0).astype(jnp.bfloat16)
+        value = jnp.concatenate([value, ones], axis=1)
+
+        def score(unit):
+            return lax.dot_general(
+                q_ref[:, unit * HD : (unit + 1) * HD],
+                key,
+                (((1,), (1,)), ((), ())),
+                preferred_element_type=jnp.float32,
+            )
+
+        following = score(0)
+        for unit in range(units):
+            scores = following
+            if unit + 1 < units:
+                following = score(unit + 1)
+            before = peak[unit]
+            top = jnp.maximum(before, jnp.max(scores, axis=1, keepdims=True))
+            peak[unit] = top
+            probs = jnp.exp2(
+                (scores - jnp.concatenate([top] * (block // HD), axis=1)) * SCALE_LOG2
+            ).astype(jnp.bfloat16)
+            fade = jnp.exp2((before - top) * SCALE_LOG2)
+            sums[unit] = sums[unit] * jnp.concatenate([fade, fade], axis=1) + jnp.dot(
+                probs, value, preferred_element_type=jnp.float32
+            )
+
+    for shard in range(shards):
+        length = lengths[shard]
+        whole = length // block
+        kv_ref = kv_refs[shard]
+
+        @pl.loop(0, whole)
+        def _(step, kv_ref=kv_ref, length=length):
+            one_block(kv_ref, pl.multiple_of(step * block, block), length, False)
+
+        @pl.when(whole * block < length)
+        def _(kv_ref=kv_ref, length=length, whole=whole):
+            one_block(kv_ref, pl.multiple_of(whole * block, block), length, True)
+
+    if finish:
+        for unit in range(units):
+            total = sums[unit]
+            out_ref[:, unit * HD : (unit + 1) * HD] = (total[:, :HD] / total[:, HD:]).astype(
+                jnp.bfloat16
+            )
+
+
+def attend(lengths, query, caches, state=None, finish=False):
+    rows, width = query.shape
+    units = width // HD
+    shards = len(caches)
+    peak = jax.ShapeDtypeStruct((units, rows, HD), jnp.float32)
+    sums = jax.ShapeDtypeStruct((units, rows, 2 * HD), jnp.float32)
+    vmem = pl.BlockSpec(memory_space=pltpu.VMEM)
+    operands = [query, *caches]
+    if state is not None:
+        operands += list(state)
+    if finish:
+        out_shape = jax.ShapeDtypeStruct(query.shape, jnp.bfloat16)
+        out_specs = vmem
+        scratch = [pltpu.VMEM(peak.shape, peak.dtype), pltpu.VMEM(sums.shape, sums.dtype)]
+    else:
+        out_shape = (peak, sums)
+        out_specs = (vmem, vmem)
+        scratch = []
+    positions = sum(cache.shape[0] for cache in caches)
+    return pl.pallas_call(
+        functools.partial(
+            attend_body,
+            shards=shards,
+            units=units,
+            resume=state is not None,
+            finish=finish,
+            block=KEY_BLOCK,
+        ),
+        out_shape=out_shape,
+        in_specs=[pl.BlockSpec(memory_space=pltpu.SMEM)] + [vmem] * len(operands),
+        out_specs=out_specs,
+        scratch_shapes=scratch,
+        compiler_params=pltpu.CompilerParams(vmem_limit_bytes=40 * 1024 * 1024),
+        cost_estimate=pl.CostEstimate(
+            flops=8 * rows * width * positions,
+            bytes_accessed=2 * rows * width + 4 * positions * HD,
+            transcendentals=rows * units * positions,
+        ),
+    )(lengths, *operands)
+
+
+def swap_pairs(size, mask):
+    return [(index, index ^ mask) for index in range(size)]
+
+
+def split_projection(query, keys, values, cache_lengths, out_weight):
+    size = lax.axis_size("aa")
+    index = lax.axis_index("aa")
+    side = index // 2
+    over = functools.partial(lax.ppermute, axis_name="aa", perm=swap_pairs(size, 2))
+    core = functools.partial(lax.ppermute, axis_name="aa", perm=swap_pairs(size, 1))
+    half = query.shape[1] // 2
+
+    def mine(array, which):
+        width = array.shape[1] // 2
+        return lax.dynamic_slice_in_dim(array, which * width, width, 1)
+
+    far_query = over(mine(query, 1 - side))
+    far_cache = over(jnp.concatenate([mine(keys, 1 - side), mine(values, 1 - side)], axis=1))
+    own_query = mine(query, side)
+    own_cache = jnp.concatenate([mine(keys, side), mine(values, side)], axis=1)
+    near_cache = core(own_cache)
+    corner_cache = core(far_cache)
+    near_length = core(cache_lengths)
+    far_length = over(cache_lengths)
+    corner_length = core(far_length)
+
+    close = jnp.concatenate([cache_lengths, near_length])
+    own_state = attend(close, own_query, [own_cache, near_cache])
+    far_state = attend(close, far_query, [own_cache, near_cache])
+    own_state = attend(far_length, own_query, [far_cache], own_state)
+    far_state = attend(far_length, far_query, [far_cache], far_state)
+    own_rows = attend(corner_length, own_query, [corner_cache], own_state, True)
+    far_rows = attend(corner_length, far_query, [corner_cache], far_state, True)
+
+    own_other = over(far_rows)
+    far_other = over(own_rows)
+    first = jnp.stack([own_rows, far_rows, core(own_rows), core(far_rows)])
+    second = jnp.stack([own_other, far_other, core(own_other), core(far_other)])
+    first_weight = lax.dynamic_slice_in_dim(out_weight, side * half, half, 0)
+    second_weight = lax.dynamic_slice_in_dim(out_weight, (1 - side) * half, half, 0)
+
+    place = lax.axis_index("ba")
+    order = jnp.array([[3, 2, 1, 0], [3, 2, 0, 1], [0, 1, 3, 2], [0, 1, 2, 3]], jnp.int32)[place]
+    slot_of = jnp.array([0, 2, 1, 3], jnp.int32)
+
+    def product(step):
+        slot = slot_of[index ^ order[step]]
+        left = lax.dynamic_index_in_dim(first, slot, 0, False)
+        right = lax.dynamic_index_in_dim(second, slot, 0, False)
+        return jnp.dot(left, first_weight, preferred_element_type=jnp.float32) + jnp.dot(
+            right, second_weight, preferred_element_type=jnp.float32
+        )
+
+    def add(one, two):
+        return (one.astype(jnp.float32) + two.astype(jnp.float32)).astype(jnp.bfloat16)
+
+    right = functools.partial(lax.ppermute, axis_name="ba")
+    left = functools.partial(lax.ppermute, axis_name="ba")
+    one = product(0).astype(jnp.bfloat16)
+    up = right(one, perm=[(0, 1)])
+    down = left(one, perm=[(3, 2)])
+    two = product(1).astype(jnp.bfloat16)
+    up = right(add(jnp.where(place == 0, two, one), up), perm=[(0, 1), (1, 2)])
+    down = left(add(jnp.where(place == 3, two, one), down), perm=[(3, 2), (2, 1)])
+    three = product(2).astype(jnp.bfloat16)
+    up = right(add(jnp.where(place == 1, two, three), up), perm=[(0, 1), (1, 2), (2, 3)])
+    down = left(add(jnp.where(place == 2, two, three), down), perm=[(3, 2), (2, 1), (1, 0)])
+    return product(3) + up.astype(jnp.float32) + down.astype(jnp.float32)
 
 
 def on_device(
@@ -67,42 +287,30 @@
     expert_up,
     expert_down,
 ):
-    heads = query.shape[1] // HD
-    own_rows = query.shape[0]
-    start_state = (
-        jnp.full((own_rows, heads), NEGATIVE, jnp.float32),
-        jnp.zeros((own_rows, heads), jnp.float32),
-        jnp.zeros((own_rows, heads * HD), jnp.float32),
-    )
-    key_piece = lax.all_gather(keys, "aa", axis=0, tiled=True)
-    value_piece = lax.all_gather(values, "aa", axis=0, tiled=True)
-    length_piece = lax.all_gather(cache_lengths, "aa", axis=0, tiled=True)
-
-    def one_shard(index, carry):
-        key_block = lax.dynamic_slice_in_dim(key_piece, index * CTX_DEV, CTX_DEV, 0)
-        value_block = lax.dynamic_slice_in_dim(value_piece, index * CTX_DEV, CTX_DEV, 0)
-        return combine_partials(
-            carry, head_partials(query, key_block, value_block, length_piece[index])
-        )
-
-    peak, total, weighted = lax.fori_loop(0, length_piece.shape[0], one_shard, start_state)
-    own = (weighted / jnp.repeat(total, HD, axis=1)).astype(jnp.bfloat16)
-    attended = lax.all_gather(own, "aa", axis=0, tiled=True)
-    hidden = residual.astype(jnp.float32) + lax.psum_scatter(
-        jnp.dot(attended, out_weight, preferred_element_type=jnp.float32).astype(jnp.bfloat16),
-        "ba",
-        scatter_dimension=0,
-        tiled=True,
-    ).astype(jnp.float32)
-    squares = lax.psum(jnp.sum(hidden * hidden, axis=1), "aa")
-    inverse = 1.0 / jnp.sqrt(squares / D + EPSILON)
-    normed = hidden * inverse[:, None] * norm_gain
-    logits = lax.psum(jnp.dot(normed, router_weight, precision=lax.Precision.HIGHEST), "aa")
+    split = (
+        lax.axis_size("aa") == 4
+        and lax.axis_size("ba") == 4
+        and keys.shape[1] == 2 * HD
+        and keys.shape[0] % KEY_BLOCK == 0
+        and query.shape[0] == residual.shape[0]
+    )
+    project = split_projection if split else plain_projection
+    hidden = residual.astype(jnp.float32) + project(
+        query, keys, values, cache_lengths, out_weight
+    )
+    width = hidden.shape[1] * lax.axis_size("aa")
     experts = router_weight.shape[1]
+    gained = hidden * norm_gain
+    squares = jnp.sum(hidden * hidden, axis=1, keepdims=True)
+    raw = jnp.dot(gained, router_weight, precision=lax.Precision.HIGHEST)
+    sums = lax.psum(jnp.concatenate([squares, raw], axis=1), "aa")
+    inverse = 1.0 / jnp.sqrt(sums[:, :1] / width + EPSILON)
+    logits = sums[:, 1:] * inverse
+    normed = gained * inverse
     chosen = expert_ids[:, None] == lax.broadcasted_iota(jnp.int32, (1, experts), 1)
     gate = jnp.sum(jnp.where(chosen, jax.nn.sigmoid(logits), 0.0), axis=1)
     expert_in = normed.astype(jnp.bfloat16)
-    slot_count = 2 * Q // (lax.axis_size("ba") * experts)
+    slot_count = 2 * query.shape[0] * lax.axis_size("aa") // (lax.axis_size("ba") * experts)
     combined = expert_ids * slot_count + expert_slots
     placing = (
         combined[:, None] == lax.broadcasted_iota(jnp.int32, (1, experts * slot_count), 1)

time: 475 us -> 392 us (0.83)
  waiting for transfers between devices: 256 us -> 183 us
  matrix products: 96 us -> 52.9 us
  Pallas kernels: 0 us -> 39.8 us
  starting transfers between devices: 5.3 us -> 29 us
  other arithmetic: 32.1 us -> 8.74 us
  between operations: 14.2 us -> 24.1 us
  local copies, waits for them, and re-layouts: 14.9 us -> 6.44 us
  blocking collectives: 50.6 us -> 44.6 us
    all_gather x3 -> x0, waiting for transfers between devices: 91.2 us -> none  [the longest x1 36.1 us: on_device(): value_piece = lax.all_gather(values, 'aa', axis=0, tiled=True)]
    ppermute x0 -> x19, waiting for transfers between devices: none -> 60.6 us  [the longest x1 26.6 us: split_projection(): far_length = over(cache_lengths)]
    reduce_scatter x1 -> x0, waiting for transfers between devices: 51.2 us -> none  [on_device(): lax.psum_scatter(jnp.dot(attended, out_weight, preferred_element_type=jnp...]
    dot_general x82 -> x9, matrix products: 60.6 us -> 15.8 us  [the longest x4 8.89 us: product(): jnp.dot(right, second_weight, preferred_element_type=jnp.float32)]
    pallas_call x0 -> x6, Pallas kernels: none -> 39.8 us  [attend(): pl.pallas_call(functools.partial(attend_body, shards=shards, units=units,...]
    ppermute x0 -> x19, starting transfers between devices: none -> 23.8 us  [the longest x1 5.96 us: split_projection(): left(add(jnp.where(place == 2, two, three), down), perm=[(3, 2), (2, 1),...]
    reduce_sum x41 -> x0, other arithmetic: 15.8 us -> none  [the longest x40 14.4 us: head_partials(): totals.append(jnp.sum(probs, axis=1))]
    add x8 -> x0, other arithmetic: 11.7 us -> none  [the longest x4 11.6 us: combine_partials(): out_one * jnp.repeat(scale_one, HD, axis=1)]
  transfers between devices with their start and end apart: 7 -> 22, of which waited for: 7 -> 10; matrix products, arithmetic and copies ran while one was open for 1% -> 4% of each run, Pallas kernels for 0% -> 9%
where the time goes in v1:
time: 392 us; the launch traced here: 388 us
  waiting for transfers between devices  183 us (47%)
  matrix products  52.9 us (13%)
  blocking collectives  44.6 us (11%)
  Pallas kernels  39.8 us (10%)
  starting transfers between devices  29 us (7%)
  between operations  24.1 us (6%)
  other arithmetic  8.74 us (2%)
  local copies, waits for them, and re-layouts  6.44 us (2%)
    reduce_scatter x1, waiting for transfers between devices, on_device(): lax.psum_scatter(lax.dot_general(down_w, act, (((0,), (1,)), ((), ())), p...  51.5 us
    all_gather x1, waiting for transfers between devices, on_device(): piece = lax.all_gather(arrived, 'aa', axis=1, tiled=True)  41.8 us
    pallas_call x6, Pallas kernels, attend(): pl.pallas_call(functools.partial(attend_body, shards=shards, units=units,...  39.8 us
    all_to_all x1, blocking collectives, on_device(): lax.all_to_all(packed, 'ba', split_axis=0, concat_axis=0, tiled=True)  38.8 us
    all_to_all x1, waiting for transfers between devices, on_device(): lax.all_to_all(expert_out, 'ba', split_axis=1, concat_axis=1, tiled=True)  29 us
    ppermute x1, waiting for transfers between devices, split_projection(): far_length = over(cache_lengths)  26.6 us
    dot_general x1, matrix products, on_device(): lax.dot_general(down_w, act, (((0,), (1,)), ((), ())), preferred_element_...  20.9 us
    dot_general x1, matrix products, on_device(): up_part = jnp.dot(piece, up_w, preferred_element_type=jnp.float32)  10.8 us
  transfers between devices with their start and end apart: 22, of which 10 were waited for; matrix products, arithmetic and copies ran while one was open for 4% of the time, Pallas kernels for 9%

profile of v1, /device:TPU:26, one launch (start us, length us, event | category | flops | bytes accessed | tf_op | source)
XLA Modules:
  0.0 388.5 jit_solution(224304677272914156)
XLA Ops:
  15.0 26.6 %collective-permute-done.refs_0_ = s32[1]{0:T(128)} collective-permute-done((s32[1]{0:T(128)}, s32[1]{0:T(128)}, u32[]{:S(2)}, u32[]{:S(2)}) %collective-permute-start) | collective-permute-done | bytes 36 | tf_op jit(solution)/shard_map/ppermute | solution.py:228
  42.7 8.7 %shard_map.148 = (f32[5,256,128]{2,1,0:T(8,128)S(1)}, f32[5,256,256]{2,1,0:T(8,128)S(1)}) custom-call(s32[2]{0:T(128)S(1)} %pad_add_fusion.refs_0_, bf16[256,640]{1,0:T(8,128)(2,1)S(1)} %collective-permute-done.6.refs_1_, bf16[2048,256]{1,0:T(8,128)(2,1)} %pad_maximum_fusion.3.refs_2_, bf16[2048,256]{1,0:T(8,128)(2,1)} %collective-permute-done.5.refs_3_), custom_call_target="tpu_custom_call" | custom-call | flops 5368709120 | bytes 2424832 | tf_op jit(solution)/shard_map/pallas_call | solution.py:183
  51.4 6.4 %shard_map.149 = (f32[5,256,128]{2,1,0:T(8,128)S(1)}, f32[5,256,256]{2,1,0:T(8,128)S(1)}) custom-call(s32[1]{0:T(128)} %collective-permute-done.refs_0_, bf16[256,640]{1,0:T(8,128)(2,1)S(1)} %collective-permute-done.6.refs_1_, bf16[2048,256]{1,0:T(8,128)(2,1)} %collective-permute-done.2.refs_2_, f32[5,256,128]{2,1,0:T(8,128)S(1)} %get-tuple-element.17.refs_3_, ...), custom_call_target="tpu_custom_call" | custom-call | flops 2684354560 | bytes 1376256 | tf_op jit(solution)/shard_map/pallas_call | solution.py:183
  57.8 8.4 %shard_map.145 = (f32[5,256,128]{2,1,0:T(8,128)S(1)}, f32[5,256,256]{2,1,0:T(8,128)S(1)}) custom-call(s32[2]{0:T(128)S(1)} %pad_add_fusion.refs_0_, bf16[256,640]{1,0:T(8,128)(2,1)S(1)} %get-tuple-element.29.refs_1_, bf16[2048,256]{1,0:T(8,128)(2,1)} %pad_maximum_fusion.3.refs_2_, bf16[2048,256]{1,0:T(8,128)(2,1)} %collective-permute-done.5.refs_3_), custom_call_target="tpu_custom_call" | custom-call | flops 5368709120 | bytes 2424832 | tf_op jit(solution)/shard_map/pallas_call | solution.py:183
  66.3 6.4 %shard_map.146 = (f32[5,256,128]{2,1,0:T(8,128)S(1)}, f32[5,256,256]{2,1,0:T(8,128)S(1)}) custom-call(s32[1]{0:T(128)} %collective-permute-done.refs_0_, bf16[256,640]{1,0:T(8,128)(2,1)S(1)} %get-tuple-element.29.refs_1_, bf16[2048,256]{1,0:T(8,128)(2,1)} %collective-permute-done.2.refs_2_, f32[5,256,128]{2,1,0:T(8,128)S(1)} %get-tuple-element.13.refs_3_, ...), custom_call_target="tpu_custom_call" | custom-call | flops 2684354560 | bytes 1376256 | tf_op jit(solution)/shard_map/pallas_call | solution.py:183
  72.7 4.9 %shard_map.150 = bf16[256,640]{1,0:T(8,128)(2,1)} custom-call(s32[1]{0:T(128)} %collective-permute-done.1.refs_0_, bf16[256,640]{1,0:T(8,128)(2,1)S(1)} %collective-permute-done.6.refs_1_, bf16[2048,256]{1,0:T(8,128)(2,1)S(1)} %collective-permute-done.3.refs_2_, f32[5,256,128]{2,1,0:T(8,128)S(1)} %get-tuple-element.19.refs_3_, ...), custom_call_target="tpu_custom_call" | custom-call | flops 2684354560 | bytes 1376256 | tf_op jit(solution)/shard_map/pallas_call | solution.py:183
  79.3 4.9 %shard_map.147 = bf16[256,640]{1,0:T(8,128)(2,1)} custom-call(s32[1]{0:T(128)} %collective-permute-done.1.refs_0_, bf16[256,640]{1,0:T(8,128)(2,1)S(1)} %get-tuple-element.29.refs_1_, bf16[2048,256]{1,0:T(8,128)(2,1)S(1)} %collective-permute-done.3.refs_2_, f32[5,256,128]{2,1,0:T(8,128)S(1)} %get-tuple-element.15.refs_3_, ...), custom_call_target="tpu_custom_call" | custom-call | flops 2684354560 | bytes 1376256 | tf_op jit(solution)/shard_map/pallas_call | solution.py:183
  87.1 6.4 %collective-permute-done.10 = bf16[256,640]{1,0:T(8,128)(2,1)} collective-permute-done((bf16[256,640]{1,0:T(8,128)(2,1)}, bf16[256,640]{1,0:T(8,128)(2,1)}, u32[]{:S(2)}, u32[]{:S(2)}) %collective-permute-start.10) | collective-permute-done | bytes 327712 | tf_op jit(solution)/shard_map/ppermute | solution.py:240
  104.7 3.2 collective-permute-start.16
  114.4 7.5 %collective-permute-done.16 = bf16[256,1280]{1,0:T(8,128)(2,1)} collective-permute-done((bf16[256,1280]{1,0:T(8,128)(2,1)}, bf16[256,1280]{1,0:T(8,128)(2,1)}, u32[]{:S(2)}, u32[]{:S(2)}) %collective-permute-start.16) | collective-permute-done | bytes 655392 | tf_op jit(solution)/shard_map/ppermute | solution.py:265
  126.4 5.0 %collective-permute-start.17 = (bf16[256,1280]{1,0:T(8,128)(2,1)}, bf16[256,1280]{1,0:T(8,128)(2,1)}, u32[]{:S(2)}, u32[]{:S(2)}) collective-permute-start(bf16[256,1280]{1,0:T(8,128)(2,1)} %get-tuple-element.24), channel_id=1, source_target_pairs={{3,2},{2,1},{7,6},{6,5},{11,10},{10,9},{15,14},{14,13},{19,18},{18... | collective-permute-start | bytes 1966088 | tf_op jit(solution)/shard_map/ppermute | solution.py:268
  134.9 9.8 %collective-permute-done.17 = bf16[256,1280]{1,0:T(8,128)(2,1)} collective-permute-done((bf16[256,1280]{1,0:T(8,128)(2,1)}, bf16[256,1280]{1,0:T(8,128)(2,1)}, u32[]{:S(2)}, u32[]{:S(2)}) %collective-permute-start.17) | collective-permute-done | bytes 655392 | tf_op jit(solution)/shard_map/ppermute | solution.py:268
  144.8 3.3 add_convert_fusion.2
  149.4 6.0 %collective-permute-start.18 = (bf16[256,1280]{1,0:T(8,128)(2,1)}, bf16[256,1280]{1,0:T(8,128)(2,1)}, u32[]{:S(2)}, u32[]{:S(2)}) collective-permute-start(bf16[256,1280]{1,0:T(8,128)(2,1)} %get-tuple-element.22), channel_id=1, source_target_pairs={{3,2},{2,1},{1,0},{7,6},{6,5},{5,4},{11,10},{10,9},{9,8},{15,14},{... | collective-permute-start | bytes 1966088 | tf_op jit(solution)/shard_map/ppermute | solution.py:271
  159.2 7.3 %collective-permute-done.15 = bf16[256,1280]{1,0:T(8,128)(2,1)} collective-permute-done((bf16[256,1280]{1,0:T(8,128)(2,1)}, bf16[256,1280]{1,0:T(8,128)(2,1)}, u32[]{:S(2)}, u32[]{:S(2)}) %collective-permute-start.15) | collective-permute-done | bytes 655392 | tf_op jit(solution)/shard_map/ppermute | solution.py:270
  172.3 5.8 %psum.7 = f32[256,5]{0,1:T(8,128)S(1)} all-reduce(f32[256,5]{0,1:T(8,128)S(1)} %pad_maximum_fusion.4), channel_id=1, replica_groups=mesh['ga'=2,'aa'=4,'ba'=4] {'aa'}, use_global_device_ids=true, to_apply=%region_1.2 | all-reduce | flops 1280 | bytes 10240 | tf_op jit(solution)/shard_map/psum | solution.py:306
  180.2 38.8 %all_to_all.24 = bf16[4,128,1280]{2,1,0:T(8,128)(2,1)} all-to-all(bf16[4,128,1280]{2,1,0:T(8,128)(2,1)S(1)} %bitcast.74), channel_id=1, replica_groups=mesh['ga'=2,'aa'=4,'ba'=4] {'ba'}, dimensions={0} | all-to-all | bytes 2621440 | tf_op jit(solution)/shard_map/all_to_all | solution.py:322
  219.1 41.8 %all-gather.2.cloned.1.call-done = bf16[512,5120]{1,0:T(8,128)(2,1)} async-done(((bf16[512,1280]{1,0:T(8,128)(2,1)}), bf16[512,5120]{1,0:T(8,128)(2,1)}) %all-gather.2.cloned.1.call-update) | async-done | bytes 5242896 | tf_op jit(solution)/shard_map/all_gather | solution.py:326
  260.9 10.8 %fusion.2 = f32[512,1024]{1,0:T(8,128)} fusion(bf16[512,5120]{1,0:T(8,128)(2,1)} %all-gather.2.cloned.1.call-done, bf16[1,5120,1024]{2,1,0:T(8,128)(2,1)} %param.26), kind=kOutput, calls=%fused_computation.2 | convolution fusion | flops 5368709120 | bytes 17825792 | tf_op jit(solution)/shard_map/dot_general | solution.py:328
  271.7 20.9 %fusion.9 = bf16[5120,512]{0,1:T(8,128)(2,1)} fusion(bf16[1,1024,5120]{2,1,0:T(8,128)(2,1)} %param.27, f32[512,1024]{1,0:T(8,128)} %fusion.2, bf16[512,5120]{1,0:T(8,128)(2,1)} %all-gather.2.cloned.1.call-done, bf16[1,5120,1024]{2,1,0:T(8,128)(2,1)} %param.25), kind=kOutput, calls=%fused_computation.7 | convolution fusion | flops 10743185408 | bytes 33554432 | tf_op jit(solution)/shard_map/dot_general | solution.py:331
  292.7 51.5 %reduce-scatter.2.cloned.1.call-done = bf16[1280,512]{0,1:T(8,128)(2,1)} async-done(((bf16[5120,512]{0,1:T(8,128)(2,1)}), bf16[1280,512]{0,1:T(8,128)(2,1)}) %reduce-scatter.2.cloned.1.call-update) | async-done | bytes 1310736 | tf_op jit(solution)/shard_map/reduce_scatter | solution.py:330
  344.2 5.1 %all-to-all-start.1 = ((bf16[1280,4,128]{0,2,1:T(8,128)(2,1)}), bf16[1280,4,128]{0,2,1:T(8,128)(2,1)}, u32[]{:S(2)}, u32[]{:S(2)}) async-start(bf16[1280,4,128]{0,2,1:T(8,128)(2,1)} %bitcast.75), calls=%async_computation.2 | async-start | bytes 2621440 | tf_op jit(solution)/shard_map/all_to_all | solution.py:338
  349.3 29.0 %all-to-all-done.1 = bf16[1280,4,128]{0,2,1:T(8,128)(2,1)} async-done(((bf16[1280,4,128]{0,2,1:T(8,128)(2,1)}), bf16[1280,4,128]{0,2,1:T(8,128)(2,1)}, u32[]{:S(2)}, u32[]{:S(2)}) %all-to-all-start.1) | async-done | bytes 1310752 | tf_op jit(solution)/shard_map/all_to_all | solution.py:338
  378.4 3.3 fusion.16
  (85 shorter events, 42.3 us)
Async XLA Ops:
  6.5 94.0 %copy-start = (bf16[1280,1280]{1,0:T(8,128)(2,1)S(1)}, bf16[1280,1280]{1,0:T(8,128)(2,1)}, u32[]{:S(2)}) copy-start(bf16[1280,1280]{1,0:T(8,128)(2,1)} %param.20) | copy-start | bytes 9830404
  6.5 254.4 %all-gather.2.cloned.1.call-start = ((), (), s32[]{:S(2)}) async-start(), calls=%async_computation.3 | async-start | bytes 6553600 | tf_op jit(solution)/shard_map/all_gather | solution.py:326
  9.4 32.8 %collective-permute-start.2 = (bf16[2048,256]{1,0:T(8,128)(2,1)}, bf16[2048,256]{1,0:T(8,128)(2,1)}, u32[]{:S(2)}, u32[]{:S(2)}) collective-permute-start(bf16[2048,256]{1,0:T(8,128)(2,1)} %pad_maximum_fusion.2), channel_id=1, source_target_pairs={{0,8},{4,12},{8,0},{12,4},{1,9},{5,13},{9,1},{13,5},{2,10},{6,14},... | collective-permute-start | bytes 3145736 | tf_op jit(solution)/shard_map/ppermute | solution.py:222
  11.1 31.7 %collective-permute-start.5 = (bf16[2048,256]{1,0:T(8,128)(2,1)}, bf16[2048,256]{1,0:T(8,128)(2,1)}, u32[]{:S(2)}, u32[]{:S(2)}) collective-permute-start(bf16[2048,256]{1,0:T(8,128)(2,1)} %pad_maximum_fusion.3.refs_2_), channel_id=1, source_target_pairs={{0,4},{4,0},{8,12},{12,8},{1,5},{5,1},{9,13},{13,9},{2,6},{6,2},{1... | collective-permute-start | bytes 3145736 | tf_op jit(solution)/shard_map/ppermute | solution.py:225
  12.2 30.5 %collective-permute-start.6 = (bf16[256,640]{1,0:T(8,128)(2,1)S(1)}, bf16[256,640]{1,0:T(8,128)(2,1)S(1)}, u32[]{:S(2)}, u32[]{:S(2)}) collective-permute-start(bf16[256,640]{1,0:T(8,128)(2,1)S(1)} %get-tuple-element.30), channel_id=1, source_target_pairs={{0,8},{4,12},{8,0},{12,4},{1,9},{5,13},{9,1},{13,5},{2,10},{6,14},... | collective-permute-start | bytes 983048 | tf_op jit(solution)/shard_map/ppermute | solution.py:221
  13.8 27.8 %collective-permute-start = (s32[1]{0:T(128)}, s32[1]{0:T(128)}, u32[]{:S(2)}, u32[]{:S(2)}) collective-permute-start(s32[1]{0:T(128)} %param.18), channel_id=1, source_target_pairs={{0,8},{4,12},{8,0},{12,4},{1,9},{5,13},{9,1},{13,5},{2,10},{6,14},... | collective-permute-start | bytes 20 | tf_op jit(solution)/shard_map/ppermute | solution.py:228
  14.3 27.3 %collective-permute-start.4 = (s32[1]{0:T(128)}, s32[1]{0:T(128)}, u32[]{:S(2)}, u32[]{:S(2)}) collective-permute-start(s32[1]{0:T(128)} %param.18), channel_id=1, source_target_pairs={{0,4},{4,0},{8,12},{12,8},{1,5},{5,1},{9,13},{13,9},{2,6},{6,2},{1... | collective-permute-start | bytes 20 | tf_op jit(solution)/shard_map/ppermute | solution.py:227
  41.6 31.1 %collective-permute-start.1 = (s32[1]{0:T(128)}, s32[1]{0:T(128)}, u32[]{:S(2)}, u32[]{:S(2)}) collective-permute-start(s32[1]{0:T(128)} %collective-permute-done.refs_0_), channel_id=1, source_target_pairs={{0,4},{4,0},{8,12},{12,8},{1,5},{5,1},{9,13},{13,9},{2,6},{6,2},{1... | collective-permute-start | bytes 20 | tf_op jit(solution)/shard_map/ppermute | solution.py:229
  42.2 30.5 %collective-permute-start.3 = (bf16[2048,256]{1,0:T(8,128)(2,1)}, bf16[2048,256]{1,0:T(8,128)(2,1)S(1)}, u32[]{:S(2)}, u32[]{:S(2)}) collective-permute-start(bf16[2048,256]{1,0:T(8,128)(2,1)} %collective-permute-done.2.refs_2_), channel_id=1, source_target_pairs={{0,4},{4,0},{8,12},{12,8},{1,5},{5,1},{9,13},{13,9},{2,6},{6,2},{1... | collective-permute-start | bytes 3145736 | tf_op jit(solution)/shard_map/ppermute | solution.py:226
  77.6 9.5 %collective-permute-start.9 = (bf16[256,640]{1,0:T(8,128)(2,1)}, bf16[256,640]{1,0:T(8,128)(2,1)}, u32[]{:S(2)}, u32[]{:S(2)}) collective-permute-start(bf16[256,640]{1,0:T(8,128)(2,1)} %shard_map.150), channel_id=1, source_target_pairs={{0,8},{4,12},{8,0},{12,4},{1,9},{5,13},{9,1},{13,5},{2,10},{6,14},... | collective-permute-start | bytes 983048 | tf_op jit(solution)/shard_map/ppermute | solution.py:239
  84.3 9.3 %collective-permute-start.10 = (bf16[256,640]{1,0:T(8,128)(2,1)}, bf16[256,640]{1,0:T(8,128)(2,1)}, u32[]{:S(2)}, u32[]{:S(2)}) collective-permute-start(bf16[256,640]{1,0:T(8,128)(2,1)} %shard_map.147), channel_id=1, source_target_pairs={{0,8},{4,12},{8,0},{12,4},{1,9},{5,13},{9,1},{13,5},{2,10},{6,14},... | collective-permute-start | bytes 983048 | tf_op jit(solution)/shard_map/ppermute | solution.py:240
  84.3 14.8 %collective-permute-start.8 = (bf16[256,640]{1,0:T(8,128)(2,1)}, bf16[256,640]{1,0:T(8,128)(2,1)}, u32[]{:S(2)}, u32[]{:S(2)}) collective-permute-start(bf16[256,640]{1,0:T(8,128)(2,1)} %shard_map.150), channel_id=1, source_target_pairs={{0,4},{4,0},{8,12},{12,8},{1,5},{5,1},{9,13},{13,9},{2,6},{6,2},{1... | collective-permute-start | bytes 983048 | tf_op jit(solution)/shard_map/ppermute | solution.py:241
  84.3 14.8 %collective-permute-start.7 = (bf16[256,640]{1,0:T(8,128)(2,1)}, bf16[256,640]{1,0:T(8,128)(2,1)}, u32[]{:S(2)}, u32[]{:S(2)}) collective-permute-start(bf16[256,640]{1,0:T(8,128)(2,1)} %shard_map.147), channel_id=1, source_target_pairs={{0,4},{4,0},{8,12},{12,8},{1,5},{5,1},{9,13},{13,9},{2,6},{6,2},{1... | collective-permute-start | bytes 983048 | tf_op jit(solution)/shard_map/ppermute | solution.py:241
  87.1 14.5 %collective-permute-start.11 = (bf16[256,640]{1,0:T(8,128)(2,1)}, bf16[256,640]{1,0:T(8,128)(2,1)}, u32[]{:S(2)}, u32[]{:S(2)}) collective-permute-start(bf16[256,640]{1,0:T(8,128)(2,1)} %collective-permute-done.9), channel_id=1, source_target_pairs={{0,4},{4,0},{8,12},{12,8},{1,5},{5,1},{9,13},{13,9},{2,6},{6,2},{1... | collective-permute-start | bytes 983048 | tf_op jit(solution)/shard_map/ppermute | solution.py:242
  93.5 8.1 %collective-permute-start.12 = (bf16[256,640]{1,0:T(8,128)(2,1)}, bf16[256,640]{1,0:T(8,128)(2,1)}, u32[]{:S(2)}, u32[]{:S(2)}) collective-permute-start(bf16[256,640]{1,0:T(8,128)(2,1)} %collective-permute-done.10), channel_id=1, source_target_pairs={{0,4},{4,0},{8,12},{12,8},{1,5},{5,1},{9,13},{13,9},{2,6},{6,2},{1... | collective-permute-start | bytes 983048 | tf_op jit(solution)/shard_map/ppermute | solution.py:242
  104.7 17.3 %collective-permute-start.16 = (bf16[256,1280]{1,0:T(8,128)(2,1)}, bf16[256,1280]{1,0:T(8,128)(2,1)}, u32[]{:S(2)}, u32[]{:S(2)}) collective-permute-start(bf16[256,1280]{1,0:T(8,128)(2,1)} %fusion.15), channel_id=1, source_target_pairs={{3,2},{7,6},{11,10},{15,14},{19,18},{23,22},{27,26},{31,30}} | collective-permute-start | bytes 1966088 | tf_op jit(solution)/shard_map/ppermute | solution.py:265
  107.9 14.1 %collective-permute-start.13 = (bf16[256,1280]{1,0:T(8,128)(2,1)}, bf16[256,1280]{1,0:T(8,128)(2,1)}, u32[]{:S(2)}, u32[]{:S(2)}) collective-permute-start(bf16[256,1280]{1,0:T(8,128)(2,1)} %fusion.15), channel_id=1, source_target_pairs={{0,1},{4,5},{8,9},{12,13},{16,17},{20,21},{24,25},{28,29}} | collective-permute-start | bytes 1966088 | tf_op jit(solution)/shard_map/ppermute | solution.py:264
  124.9 10.0 %collective-permute-start.14 = (bf16[256,1280]{1,0:T(8,128)(2,1)}, bf16[256,1280]{1,0:T(8,128)(2,1)}, u32[]{:S(2)}, u32[]{:S(2)}) collective-permute-start(bf16[256,1280]{1,0:T(8,128)(2,1)} %get-tuple-element.23), channel_id=1, source_target_pairs={{0,1},{1,2},{4,5},{5,6},{8,9},{9,10},{12,13},{13,14},{16,17},{17,1... | collective-permute-start | bytes 1966088 | tf_op jit(solution)/shard_map/ppermute | solution.py:267
  126.4 18.3 %collective-permute-start.17 = (bf16[256,1280]{1,0:T(8,128)(2,1)}, bf16[256,1280]{1,0:T(8,128)(2,1)}, u32[]{:S(2)}, u32[]{:S(2)}) collective-permute-start(bf16[256,1280]{1,0:T(8,128)(2,1)} %get-tuple-element.24), channel_id=1, source_target_pairs={{3,2},{2,1},{7,6},{6,5},{11,10},{10,9},{15,14},{14,13},{19,18},{18... | collective-permute-start | bytes 1966088 | tf_op jit(solution)/shard_map/ppermute | solution.py:268
  134.9 22.5 %copy-start.11 = (s32[256]{0:T(256)S(1)}, s32[256]{0:T(256)}, u32[]{:S(2)}) copy-start(s32[256]{0:T(256)} %param.23) | copy-start | bytes 3076
  148.1 18.5 %collective-permute-start.15 = (bf16[256,1280]{1,0:T(8,128)(2,1)}, bf16[256,1280]{1,0:T(8,128)(2,1)}, u32[]{:S(2)}, u32[]{:S(2)}) collective-permute-start(bf16[256,1280]{1,0:T(8,128)(2,1)} %get-tuple-element.21), channel_id=1, source_target_pairs={{0,1},{1,2},{2,3},{4,5},{5,6},{6,7},{8,9},{9,10},{10,11},{12,13},{... | collective-permute-start | bytes 1966088 | tf_op jit(solution)/shard_map/ppermute | solution.py:270
  149.4 18.3 %collective-permute-start.18 = (bf16[256,1280]{1,0:T(8,128)(2,1)}, bf16[256,1280]{1,0:T(8,128)(2,1)}, u32[]{:S(2)}, u32[]{:S(2)}) collective-permute-start(bf16[256,1280]{1,0:T(8,128)(2,1)} %get-tuple-element.22), channel_id=1, source_target_pairs={{3,2},{2,1},{1,0},{7,6},{6,5},{5,4},{11,10},{10,9},{9,8},{15,14},{... | collective-permute-start | bytes 1966088 | tf_op jit(solution)/shard_map/ppermute | solution.py:271
  219.0 125.2 %reduce-scatter.2.cloned.1.call-start = ((), (), s32[]{:S(2)}) async-start(), calls=%async_computation.4 | async-start | bytes 6553600 | tf_op jit(solution)/shard_map/reduce_scatter | solution.py:330
  344.2 34.2 %all-to-all-start.1 = ((bf16[1280,4,128]{0,2,1:T(8,128)(2,1)}), bf16[1280,4,128]{0,2,1:T(8,128)(2,1)}, u32[]{:S(2)}, u32[]{:S(2)}) async-start(bf16[1280,4,128]{0,2,1:T(8,128)(2,1)} %bitcast.75), calls=%async_computation.2 | async-start | bytes 2621440 | tf_op jit(solution)/shard_map/all_to_all | solution.py:338
  (11 other events, 103.1 us)
Sparse Core Ops, SparseCore 0:
  219.2 41.7 all-gather.1
  292.8 51.3 reduce-scatter.1
